TPU v7x, 32 devices: a whole 2x2x4 slice. The times are simulated.
32 devices in a mesh: groups: 2 (over x), beam: 16 (over z, y, core).
Axes of the slice: x: 2, y: 2, z: 4, core: 2. Of those that a mesh axis runs over, the one named last changes fastest.
Arguments:
- transmission: float32 [2, 2, 512, 512], P('groups'), parts along dimension 0, may hold values from -1 to 1, as said below
- beams: int32 [16, 2], P('beam'), may hold values from -64 to 63
- phases: int32 [32, 16], replicated, may hold values from 0 to 63
- positions: int32 [32, 2], replicated, may hold values from 0 to 128
- owner: int32 [32], replicated, may hold values from 0 to 15, as said below
Outputs:
- patterns: float32 [128, 128, 128], P(('groups', 'beam')), parts along dimension 0
There are 2 independent parts, one for each index of `groups`. A program takes and returns all parts, laid end to end along the dimension named above; an argument that names none is the same for every part. Nothing has to cross between parts.
Inputs may be any that keep to these rules, and one draw needn't show every extreme that they name: `transmission`: real and imaginary parts of each pixel form a pair of magnitude at most 1. Each owner is given at most 4 probes, and some owner exactly 4.
All inputs are finite; a program needn't handle non-finite values.
Results may differ from a plain program's by a relative error of at most 0.0003.
Values sent between devices are 32-bit elements; how exact they have to be, the bound alone decides.
A program may use at most 64 MiB of HBM per device.

v0:
```python
import functools
import math

import jax
import jax.numpy as jnp
import ml_dtypes
import numpy as np
from jax import lax
from jax.experimental import pallas as pl
from jax.experimental.pallas import tpu as pltpu
from jax.sharding import PartitionSpec as P

GRID = 512
CROP = 256
WINDOW = 128
LEVELS = 64
CAP = 4
TEAM = 8
CHUNK = 16

bf16 = jnp.bfloat16
f32 = jnp.float32
MESH = pl.DeviceIdType.MESH


def host_split(x):
    x = np.asarray(x, np.float32)
    hi = x.astype(ml_dtypes.bfloat16)
    lo = (x - hi.astype(np.float32)).astype(ml_dtypes.bfloat16)
    return hi, lo


def constants(length, team):
    index = np.arange(length)
    freq = np.where(index < length // 2, index, index - length)
    chirp = np.exp(-1j * 0.0004 * np.pi * freq.astype(np.float64) ** 2)
    kernel = np.fft.ifft(chirp)
    rows = (length - CROP) // 2 + np.arange(CROP)
    step = kernel[(rows[:, None] - index[None, :]) % length]
    dealt = step.reshape(CROP // team, team, length).transpose(1, 0, 2)
    a = np.stack([dealt.real, dealt.imag], axis=1).astype(np.float32)
    st = step.T
    b = np.block([[st.real, st.imag], [-st.imag, st.real]])
    w = np.arange(WINDOW)
    ang = 2 * np.pi * ((w[:, None] * w[None, :]) % WINDOW) / WINDOW
    c, s = np.cos(ang), np.sin(ang)
    x = np.block([[c, -s], [s, c]])
    order = w.reshape(WINDOW // team, team).T.reshape(-1)
    y = np.concatenate([c[:, order], s[:, order]], axis=0)
    return a, host_split(b), host_split(x), host_split(y)


def split(x):
    hi = x.astype(bf16)
    return hi, (x - hi.astype(f32)).astype(bf16)


def dot(a, b):
    return jnp.dot(a, b, preferred_element_type=f32)


def dot3(ah, al, bh, bl):
    return dot(ah, bh) + (dot(ah, bl) + dot(al, bh))


def kernel(n, team, chunk,
           t_ref, beams_ref, phases_ref, pos_ref, owner_ref, a_ref, bh_ref, bl_ref,
           xh_ref, xl_ref, yh_ref, yl_ref, out_ref,
           kmine, kbuf, th, tl, lh, ll, s_buf, eh, el, wh, wl, p_buf, xbuf, zbuf,
           ksend, krecv, xsend, xrecv):
    length = t_ref.shape[1]
    probes, beams = phases_ref.shape
    hold = CROP // team
    fold = WINDOW // team
    m = chunk * hold
    slots = team * CAP
    sj = slots * fold
    me = lax.axis_index("beam")
    mi = lax.rem(me, team)
    base = me - mi

    barrier = pltpu.get_barrier_semaphore()
    for d in range(1, n):
        pl.semaphore_signal(barrier, inc=1, device_id={"beam": lax.rem(me + d, n)}, device_id_type=MESH)
    half = lax.broadcasted_iota(jnp.int32, (8, 128), 0) < 4
    kmine[...] = jnp.where(half, beams_ref[0:1, 0:1], beams_ref[0:1, 1:2])
    kbuf[me] = kmine[...]
    pl.semaphore_wait(barrier, n - 1)
    sends = []
    for d in range(1, n):
        copy = pltpu.make_async_remote_copy(
            src_ref=kmine, dst_ref=kbuf.at[me], send_sem=ksend.at[d - 1], recv_sem=krecv.at[d - 1],
            device_id={"beam": lax.rem(me + d, n)}, device_id_type=MESH)
        copy.start()
        sends.append(copy)

    t_hi, t_lo = split(t_ref[...])
    th[...] = t_hi
    tl[...] = t_lo
    owner_row = owner_ref[...].astype(f32)
    pi = lax.broadcasted_iota(jnp.int32, (probes, probes), 0)
    pj = lax.broadcasted_iota(jnp.int32, (probes, probes), 1)
    owner_col = jnp.sum(jnp.where(pi == pj, owner_row, 0.0), axis=1, keepdims=True)
    rank = jnp.sum(jnp.where((owner_col == owner_row) & (pi < pj), 1.0, 0.0), axis=0, keepdims=True)
    target = owner_row * CAP + rank
    slot_id = (lax.broadcasted_iota(jnp.int32, (slots, probes), 0) + base * CAP).astype(f32)
    hit = jnp.where(target == slot_id, 1.0, 0.0)
    used = jnp.sum(hit, axis=1, keepdims=True)
    hit16 = hit.astype(bf16)
    place = dot(hit16, pos_ref[...].astype(f32).astype(bf16))
    level = dot(hit16, phases_ref[...].astype(f32).astype(bf16)).astype(bf16)

    def rows_of(x):
        return jnp.broadcast_to(x[:, None, :], (slots, fold, x.shape[-1])).reshape(sj, x.shape[-1])

    top = rows_of(jnp.broadcast_to(place[:, 0:1], (slots, 128)))[:, 0:1]
    left = rows_of(jnp.broadcast_to(place[:, 1:2], (slots, 128)))
    j_row = lax.broadcasted_iota(jnp.int32, (sj, 1), 0) & (fold - 1)
    first = (j_row * team + mi).astype(f32)
    pick = j_row + jnp.where(first < top, fold, 0)

    for copy in sends:
        copy.wait_recv()

    def one_chunk(c, is_first):
        bi = lax.broadcasted_iota(jnp.int32, (beams, m), 0)
        bj = lax.broadcasted_iota(jnp.int32, (beams, m), 1)
        spread = jnp.where(bi == c * chunk + bj // hold, 1.0, 0.0).astype(bf16)
        angle = dot(level, spread) * (2.0 * math.pi / LEVELS)
        scale = used * (1.0 / math.sqrt(beams))
        keep = (lax.broadcasted_iota(jnp.int32, (sj, m), 1) & (hold - 1)) == pick
        w_hi, w_lo = split(jnp.where(keep, rows_of(jnp.cos(angle) * scale), 0.0))
        wh[0:sj] = w_hi
        wl[0:sj] = w_lo
        w_hi, w_lo = split(jnp.where(keep, rows_of(jnp.sin(angle) * scale), 0.0))
        wh[sj:] = w_hi
        wl[sj:] = w_lo

        index = lax.broadcasted_iota(jnp.int32, (chunk, length), 1)

        def wave(row):
            k = kbuf[pl.ds(c * chunk, chunk), row, :]
            k = jnp.concatenate([k] * (length // 128), axis=1)
            ang = ((k * index) & (length - 1)).astype(f32) * (2.0 * math.pi / length)
            return jnp.cos(ang)[:, None, :], jnp.sin(ang)[:, None, :]

        cy, sy = wave(0)
        cx, sx = wave(4)
        ar = a_ref[mi, 0][None]
        ai = a_ref[mi, 1][None]
        lr_hi, lr_lo = split((ar * cy - ai * sy).reshape(m, length))
        li_hi, li_lo = split((ar * sy + ai * cy).reshape(m, length))
        lh[0:m, 0:length] = lr_hi
        ll[0:m, 0:length] = lr_lo
        lh[0:m, length:] = -li_hi
        ll[0:m, length:] = -li_lo
        lh[m:, 0:length] = li_hi
        ll[m:, 0:length] = li_lo
        lh[m:, length:] = lr_hi
        ll[m:, length:] = lr_lo

        @pl.loop(0, length // 256)
        def _(q):
            cols = pl.ds(pl.multiple_of(q * 256, 256), 256)
            s_buf[:, cols] = dot3(lh[...], ll[...], th[:, cols], tl[:, cols])

        sr = s_buf[0:m].reshape(chunk, hold, length)
        si = s_buf[m:].reshape(chunk, hold, length)
        hi, lo = split((sr * cx - si * sx).reshape(m, length))
        lh[0:m, 0:length] = hi
        ll[0:m, 0:length] = lo
        hi, lo = split((sr * sx + si * cx).reshape(m, length))
        lh[0:m, length:] = hi
        ll[0:m, length:] = lo

        @pl.loop(0, 2 * CROP // 256)
        def _(q):
            cols = pl.ds(pl.multiple_of(q * 256, 256), 256)
            hi, lo = split(dot3(lh[0:m], ll[0:m], bh_ref[:, cols], bl_ref[:, cols]))
            eh[:, cols] = hi
            el[:, cols] = lo

        @pl.loop(0, 2 * CROP // 256)
        def _(q):
            cols = pl.ds(pl.multiple_of(q * 256, 256), 256)
            part = dot3(wh[...], wl[...], eh[:, cols], el[:, cols])
            p_buf[:, cols] = part if is_first else p_buf[:, cols] + part

    one_chunk(0, True)
    if beams > chunk:
        @pl.loop(1, beams // chunk)
        def _(c):
            one_chunk(c, False)

    vr = p_buf[0:sj, 0:CROP] - p_buf[sj:, CROP:]
    vi = p_buf[0:sj, CROP:] + p_buf[sj:, 0:CROP]
    inside = lax.broadcasted_iota(jnp.int32, (sj, WINDOW), 1).astype(f32) >= left
    folded = jnp.concatenate(
        [jnp.where(inside, vr[:, 0:WINDOW], vr[:, WINDOW:]),
         jnp.where(inside, vi[:, 0:WINDOW], vi[:, WINDOW:])], axis=1)
    f_hi, f_lo = split(folded)
    xbuf[...] = dot3(f_hi, f_lo, xh_ref[...], xl_ref[...]).reshape(team, CAP * fold, 2 * WINDOW)

    copies = []
    for e in range(1, team):
        other = lax.rem(mi + e, team)
        copy = pltpu.make_async_remote_copy(
            src_ref=xbuf.at[other], dst_ref=zbuf.at[mi], send_sem=xsend.at[e - 1], recv_sem=xrecv.at[e - 1],
            device_id={"beam": base + other}, device_id_type=MESH)
        copy.start()
        copies.append(copy)
    zbuf[mi] = xbuf[mi]
    for copy in copies:
        copy.wait_recv()
    for k in range(CAP):
        z = zbuf[:, k * fold:(k + 1) * fold, :].reshape(WINDOW, 2 * WINDOW)
        z_hi, z_lo = split(z)
        y = dot3(yh_ref[...], yl_ref[...], z_hi, z_lo)
        yr = y[0:WINDOW, 0:WINDOW] + y[WINDOW:, WINDOW:]
        yi = y[0:WINDOW, WINDOW:] - y[WINDOW:, 0:WINDOW]
        out_ref[k] = (yr * yr + yi * yi) * (1.0 / (WINDOW * WINDOW))
    for copy in sends + copies:
        copy.wait_send()


def solution(mesh):
    n = mesh.shape["beam"]
    team = math.gcd(n, TEAM)

    def local(transmission, beams, phases, positions, owner):
        length = transmission.shape[-1]
        probes, beam_total = phases.shape
        chunk = math.gcd(beam_total, CHUNK)
        a, b, x, y = constants(length, team)
        m = chunk * (CROP // team)
        sj = CAP * WINDOW
        t = transmission.reshape(2 * length, length)
        return pl.pallas_call(
            functools.partial(kernel, n, team, chunk),
            out_shape=jax.ShapeDtypeStruct((CAP, WINDOW, WINDOW), f32),
            in_specs=[pl.BlockSpec(memory_space=pltpu.VMEM)] * 12,
            out_specs=pl.BlockSpec(memory_space=pltpu.VMEM),
            scratch_shapes=[
                pltpu.VMEM((8, 128), jnp.int32),
                pltpu.VMEM((n, 8, 128), jnp.int32),
                pltpu.VMEM((2 * length, length), bf16),
                pltpu.VMEM((2 * length, length), bf16),
                pltpu.VMEM((2 * m, 2 * length), bf16),
                pltpu.VMEM((2 * m, 2 * length), bf16),
                pltpu.VMEM((2 * m, length), f32),
                pltpu.VMEM((m, 2 * CROP), bf16),
                pltpu.VMEM((m, 2 * CROP), bf16),
                pltpu.VMEM((2 * sj, m), bf16),
                pltpu.VMEM((2 * sj, m), bf16),
                pltpu.VMEM((2 * sj, 2 * CROP), f32),
                pltpu.VMEM((team, CAP * WINDOW // team, 2 * WINDOW), f32),
                pltpu.VMEM((team, CAP * WINDOW // team, 2 * WINDOW), f32),
                pltpu.SemaphoreType.DMA((n - 1,)),
                pltpu.SemaphoreType.DMA((n - 1,)),
                pltpu.SemaphoreType.DMA((team - 1,)),
                pltpu.SemaphoreType.DMA((team - 1,)),
            ],
            compiler_params=pltpu.CompilerParams(
                collective_id=0, has_side_effects=True, vmem_limit_bytes=48 << 20),
        )(t, beams, phases, positions, owner.reshape(1, probes), a, *b, *x, *y)

    in_specs = (P("groups", None, None, None), P("beam", None), P(), P(), P())
    out_specs = P(("groups", "beam"), None, None)
    return jax.shard_map(local, mesh=mesh, in_specs=in_specs, out_specs=out_specs, check_vma=False)
```

profile of v0, /device:TPU:1, one launch (start us, length us, event | category | flops | bytes accessed | tf_op | source)
XLA Modules:
  0.0 40.8 jit_solution(9346297304648627578)
XLA Ops:
  0.0 0.8 %copy.13.phases_ref = s32[32,16]{1,0:T(8,128)S(1)} copy(s32[32,16]{0,1:T(8,128)} %param.14) | data formatting | bytes 4096 | tf_op args[2]
  0.8 0.8 %copy.14.pos_ref = s32[32,2]{1,0:T(8,128)S(1)} copy(s32[32,2]{0,1:T(2,128)} %param.15) | data formatting | bytes 512 | tf_op args[3]
  1.5 0.0 copy-start
  1.5 1.6 %copy-done = f32[1,2,512,512]{3,2,1,0:T(8,128)S(1)} copy-done((f32[1,2,512,512]{3,2,1,0:T(8,128)S(1)}, f32[1,2,512,512]{3,2,1,0:T(8,128)}, u32[]{:S(2)}) %copy-start) | copy-done | bytes 2097176
  3.1 0.0 copy-start.1
  3.1 1.2 %copy-done.1 = bf16[1024,512]{1,0:T(8,128)(2,1)S(1)} copy-done((bf16[1024,512]{1,0:T(8,128)(2,1)S(1)}, bf16[1024,512]{1,0:T(8,128)(2,1)}, u32[]{:S(2)}) %copy-start.1) | copy-done | bytes 1048600
  4.3 0.0 copy-start.2
  4.4 1.2 %copy-done.2 = bf16[1024,512]{1,0:T(8,128)(2,1)S(1)} copy-done((bf16[1024,512]{1,0:T(8,128)(2,1)S(1)}, bf16[1024,512]{1,0:T(8,128)(2,1)}, u32[]{:S(2)}) %copy-start.2) | copy-done | bytes 1048600
  5.6 0.0 copy-start.3
  5.6 1.2 %copy-done.3 = f32[8,2,32,512]{3,2,1,0:T(8,128)S(1)} copy-done((f32[8,2,32,512]{3,2,1,0:T(8,128)S(1)}, f32[8,2,32,512]{3,2,1,0:T(8,128)}, u32[]{:S(2)}) %copy-start.3) | copy-done | bytes 1048600
  6.8 0.0 copy-start.4
  6.8 0.9 %copy-done.4 = bf16[256,256]{1,0:T(8,128)(2,1)S(1)} copy-done((bf16[256,256]{1,0:T(8,128)(2,1)S(1)}, bf16[256,256]{1,0:T(8,128)(2,1)}, u32[]{:S(2)}) %copy-start.4) | copy-done | bytes 131096
  7.7 0.0 copy-start.5
  7.7 0.9 %copy-done.5 = bf16[256,256]{1,0:T(8,128)(2,1)S(1)} copy-done((bf16[256,256]{1,0:T(8,128)(2,1)S(1)}, bf16[256,256]{1,0:T(8,128)(2,1)}, u32[]{:S(2)}) %copy-start.5) | copy-done | bytes 131096
  8.6 0.0 copy-start.6
  8.6 0.8 %copy-done.6 = bf16[256,128]{1,0:T(8,128)(2,1)S(1)} copy-done((bf16[256,128]{1,0:T(8,128)(2,1)S(1)}, bf16[256,128]{1,0:T(8,128)(2,1)}, u32[]{:S(2)}) %copy-start.6) | copy-done | bytes 65560
  9.4 0.0 copy-start.7
  9.5 0.8 %copy-done.7 = bf16[256,128]{1,0:T(8,128)(2,1)S(1)} copy-done((bf16[256,128]{1,0:T(8,128)(2,1)S(1)}, bf16[256,128]{1,0:T(8,128)(2,1)}, u32[]{:S(2)}) %copy-start.7) | copy-done | bytes 65560
  10.3 0.0 copy-start.8
  10.3 0.7 %copy-done.8 = s32[1,2]{1,0:T(1,128)S(1)} copy-done((s32[1,2]{1,0:T(1,128)S(1)}, s32[1,2]{1,0:T(1,128)}, u32[]{:S(2)}) %copy-start.8) | copy-done | bytes 32
  10.9 0.0 copy-start.9
  10.9 0.7 %copy-done.9 = s32[32]{0:T(128)S(1)} copy-done((s32[32]{0:T(128)S(1)}, s32[32]{0:T(128)}, u32[]{:S(2)}) %copy-start.9) | copy-done | bytes 152
  11.6 28.5 %shard_map.118 = f32[4,128,128]{2,1,0:T(8,128)S(1)} custom-call(f32[1024,512]{1,0:T(8,128)S(1)} %bitcast.2, s32[1,2]{1,0:T(1,128)S(1)} %copy-done.8, s32[32,16]{1,0:T(8,128)S(1)} %copy.13.phases_ref, s32[32,2]{1,0:T(8,128)S(1)} %copy.14.pos_ref, s32[1,32]{1,0:T(1,128)S(1)} %bitcast.3, f32[8,2,32,512]{3,2,1,0:T(8,128)S(1)} %copy-done.3, ...), custom_call_target="tpu_custom_call" | custom-call | tf_op jit(solution)/shard_map/pallas_call | solution.py:238
  40.1 0.7 %copy.16 = f32[4,128,128]{2,1,0:T(8,128)} copy(f32[4,128,128]{2,1,0:T(8,128)S(1)} %shard_map.118) | data formatting | bytes 524288
Async XLA Ops:
  1.5 1.6 %copy-start = (f32[1,2,512,512]{3,2,1,0:T(8,128)S(1)}, f32[1,2,512,512]{3,2,1,0:T(8,128)}, u32[]{:S(2)}) copy-start(f32[1,2,512,512]{3,2,1,0:T(8,128)} %param.12) | copy-start | bytes 6291460
  3.1 1.2 %copy-start.1 = (bf16[1024,512]{1,0:T(8,128)(2,1)S(1)}, bf16[1024,512]{1,0:T(8,128)(2,1)}, u32[]{:S(2)}) copy-start(bf16[1024,512]{1,0:T(8,128)(2,1)} %constant.16.clone.bl_ref) | copy-start | bytes 3145732
  4.3 1.2 %copy-start.2 = (bf16[1024,512]{1,0:T(8,128)(2,1)S(1)}, bf16[1024,512]{1,0:T(8,128)(2,1)}, u32[]{:S(2)}) copy-start(bf16[1024,512]{1,0:T(8,128)(2,1)} %constant.15.clone.bh_ref) | copy-start | bytes 3145732
  5.6 1.2 %copy-start.3 = (f32[8,2,32,512]{3,2,1,0:T(8,128)S(1)}, f32[8,2,32,512]{3,2,1,0:T(8,128)}, u32[]{:S(2)}) copy-start(f32[8,2,32,512]{3,2,1,0:T(8,128)} %constant.14.clone.a_ref) | copy-start | bytes 3145732
  6.8 0.9 %copy-start.4 = (bf16[256,256]{1,0:T(8,128)(2,1)S(1)}, bf16[256,256]{1,0:T(8,128)(2,1)}, u32[]{:S(2)}) copy-start(bf16[256,256]{1,0:T(8,128)(2,1)} %constant.18.clone.xl_ref) | copy-start | bytes 393220
  7.7 0.9 %copy-start.5 = (bf16[256,256]{1,0:T(8,128)(2,1)S(1)}, bf16[256,256]{1,0:T(8,128)(2,1)}, u32[]{:S(2)}) copy-start(bf16[256,256]{1,0:T(8,128)(2,1)} %constant.17.clone.xh_ref) | copy-start | bytes 393220
  8.6 0.8 %copy-start.6 = (bf16[256,128]{1,0:T(8,128)(2,1)S(1)}, bf16[256,128]{1,0:T(8,128)(2,1)}, u32[]{:S(2)}) copy-start(bf16[256,128]{1,0:T(8,128)(2,1)} %constant.20.clone.yl_ref) | copy-start | bytes 196612
  9.4 0.8 %copy-start.7 = (bf16[256,128]{1,0:T(8,128)(2,1)S(1)}, bf16[256,128]{1,0:T(8,128)(2,1)}, u32[]{:S(2)}) copy-start(bf16[256,128]{1,0:T(8,128)(2,1)} %constant.19.clone.yh_ref) | copy-start | bytes 196612
  10.3 0.7 %copy-start.8 = (s32[1,2]{1,0:T(1,128)S(1)}, s32[1,2]{1,0:T(1,128)}, u32[]{:S(2)}) copy-start(s32[1,2]{1,0:T(1,128)} %beams_ref.1) | copy-start | bytes 28
  10.9 0.7 %copy-start.9 = (s32[32]{0:T(128)S(1)}, s32[32]{0:T(128)}, u32[]{:S(2)}) copy-start(s32[32]{0:T(128)} %param.16) | copy-start | bytes 388
where the time goes:
time: 41.3 us; the launch traced here: 40.8 us
  Pallas kernels  28.5 us (69%)
  local copies, waits for them, and re-layouts  12.3 us (30%)
    pallas_call x1, Pallas kernels, local(): pl.pallas_call(functools.partial(kernel, n, team, chunk), out_shape=jax.S...  28.5 us
    unnamed x23, local copies, waits for them, and re-layouts  12.3 us

commit v1 on v0

--- a/solution.py
+++ b/solution.py
@@ -59,17 +59,23 @@
     return jnp.dot(a, b, preferred_element_type=f32)
 
 
+def dot_t(a, b):
+    return lax.dot_general(a, b, (((1,), (1,)), ((), ())), preferred_element_type=f32)
+
+
 def dot3(ah, al, bh, bl):
     return dot(ah, bh) + (dot(ah, bl) + dot(al, bh))
 
 
 def kernel(n, team, chunk,
+           t_hbm, beams_hbm, phases_hbm, pos_hbm, owner_hbm, a_hbm, bh_hbm, bl_hbm,
+           xh_hbm, xl_hbm, yh_hbm, yl_hbm, out_ref,
            t_ref, beams_ref, phases_ref, pos_ref, owner_ref, a_ref, bh_ref, bl_ref,
-           xh_ref, xl_ref, yh_ref, yl_ref, out_ref,
+           xh_ref, xl_ref, yh_ref, yl_ref, fetch,
            kmine, kbuf, th, tl, lh, ll, s_buf, eh, el, wh, wl, p_buf, xbuf, zbuf,
            ksend, krecv, xsend, xrecv):
     length = t_ref.shape[1]
-    probes, beams = phases_ref.shape
+    beams, probes = phases_ref.shape
     hold = CROP // team
     fold = WINDOW // team
     m = chunk * hold
@@ -79,9 +85,17 @@
     mi = lax.rem(me, team)
     base = me - mi
 
+    moves = [
+        pltpu.make_async_copy(src, dst, fetch.at[i]) for i, (src, dst) in enumerate((
+            (beams_hbm, beams_ref), (owner_hbm, owner_ref), (phases_hbm, phases_ref), (pos_hbm, pos_ref),
+            (t_hbm, t_ref), (a_hbm.at[mi], a_ref), (bh_hbm, bh_ref), (bl_hbm, bl_ref),
+            (xh_hbm, xh_ref), (xl_hbm, xl_ref), (yh_hbm, yh_ref), (yl_hbm, yl_ref)))]
+    for move in moves:
+        move.start()
     barrier = pltpu.get_barrier_semaphore()
     for d in range(1, n):
         pl.semaphore_signal(barrier, inc=1, device_id={"beam": lax.rem(me + d, n)}, device_id_type=MESH)
+    moves[0].wait()
     half = lax.broadcasted_iota(jnp.int32, (8, 128), 0) < 4
     kmine[...] = jnp.where(half, beams_ref[0:1, 0:1], beams_ref[0:1, 1:2])
     kbuf[me] = kmine[...]
@@ -94,9 +108,8 @@
         copy.start()
         sends.append(copy)
 
-    t_hi, t_lo = split(t_ref[...])
-    th[...] = t_hi
-    tl[...] = t_lo
+    for move in moves[1:4]:
+        move.wait()
     owner_row = owner_ref[...].astype(f32)
     pi = lax.broadcasted_iota(jnp.int32, (probes, probes), 0)
     pj = lax.broadcasted_iota(jnp.int32, (probes, probes), 1)
@@ -107,8 +120,8 @@
     hit = jnp.where(target == slot_id, 1.0, 0.0)
     used = jnp.sum(hit, axis=1, keepdims=True)
     hit16 = hit.astype(bf16)
-    place = dot(hit16, pos_ref[...].astype(f32).astype(bf16))
-    level = dot(hit16, phases_ref[...].astype(f32).astype(bf16)).astype(bf16)
+    place = dot_t(hit16, pos_ref[...].astype(f32).astype(bf16))
+    level = dot_t(hit16, phases_ref[...].astype(f32).astype(bf16)).astype(bf16)
 
     def rows_of(x):
         return jnp.broadcast_to(x[:, None, :], (slots, fold, x.shape[-1])).reshape(sj, x.shape[-1])
@@ -119,6 +132,12 @@
     first = (j_row * team + mi).astype(f32)
     pick = j_row + jnp.where(first < top, fold, 0)
 
+    moves[4].wait()
+    t_hi, t_lo = split(t_ref[...])
+    th[...] = t_hi
+    tl[...] = t_lo
+    for move in moves[5:]:
+        move.wait()
     for copy in sends:
         copy.wait_recv()
 
@@ -146,8 +165,8 @@
 
         cy, sy = wave(0)
         cx, sx = wave(4)
-        ar = a_ref[mi, 0][None]
-        ai = a_ref[mi, 1][None]
+        ar = a_ref[0][None]
+        ai = a_ref[1][None]
         lr_hi, lr_lo = split((ar * cy - ai * sy).reshape(m, length))
         li_hi, li_lo = split((ar * sy + ai * cy).reshape(m, length))
         lh[0:m, 0:length] = lr_hi
@@ -235,12 +254,15 @@
         m = chunk * (CROP // team)
         sj = CAP * WINDOW
         t = transmission.reshape(2 * length, length)
+        operands = (t, beams, phases.T, positions.T, owner.reshape(1, probes), a, *b, *x, *y)
+        held = [pltpu.VMEM(v.shape[1:] if v is a else v.shape, v.dtype) for v in operands]
         return pl.pallas_call(
             functools.partial(kernel, n, team, chunk),
             out_shape=jax.ShapeDtypeStruct((CAP, WINDOW, WINDOW), f32),
-            in_specs=[pl.BlockSpec(memory_space=pltpu.VMEM)] * 12,
+            in_specs=[pl.BlockSpec(memory_space=pl.ANY)] * 12,
             out_specs=pl.BlockSpec(memory_space=pltpu.VMEM),
-            scratch_shapes=[
+            scratch_shapes=held + [
+                pltpu.SemaphoreType.DMA((len(operands),)),
                 pltpu.VMEM((8, 128), jnp.int32),
                 pltpu.VMEM((n, 8, 128), jnp.int32),
                 pltpu.VMEM((2 * length, length), bf16),
@@ -261,8 +283,8 @@
                 pltpu.SemaphoreType.DMA((team - 1,)),
             ],
             compiler_params=pltpu.CompilerParams(
-                collective_id=0, has_side_effects=True, vmem_limit_bytes=48 << 20),
-        )(t, beams, phases, positions, owner.reshape(1, probes), a, *b, *x, *y)
+                collective_id=0, has_side_effects=True, vmem_limit_bytes=60 << 20),
+        )(*operands)
 
     in_specs = (P("groups", None, None, None), P("beam", None), P(), P(), P())
     out_specs = P(("groups", "beam"), None, None)

time: 41.3 us -> 31.2 us (0.76)
  local copies, waits for them, and re-layouts: 12.3 us -> 1.67 us
  Pallas kernels: 28.5 us -> 29.4 us
    unnamed x23 -> x1, local copies, waits for them, and re-layouts: 12.3 us -> 1.67 us
    pallas_call x1, Pallas kernels: 28.5 us -> 29.4 us  [local(): pl.pallas_call(functools.partial(kernel, n, team, chunk), out_shape=jax.S...]
where the time goes in v1:
time: 31.2 us; the launch traced here: 31.1 us
  Pallas kernels  29.4 us (94%)
  local copies, waits for them, and re-layouts  1.67 us (5%)
    pallas_call x1, Pallas kernels, local(): pl.pallas_call(functools.partial(kernel, n, team, chunk), out_shape=jax.S...  29.4 us
    unnamed x1, local copies, waits for them, and re-layouts  1.67 us

profile of v1, /device:TPU:1, one launch (start us, length us, event | category | flops | bytes accessed | tf_op | source)
XLA Modules:
  0.0 31.1 jit_solution(18360199218230083260)
XLA Ops:
  0.0 29.4 %shard_map.118 = f32[4,128,128]{2,1,0:T(8,128)} custom-call(f32[1024,512]{1,0:T(8,128)} %bitcast.4, s32[1,2]{1,0:T(1,128)} %beams_hbm.1, s32[16,32]{1,0:T(8,128)} %bitcast.5, s32[2,32]{1,0:T(2,128)} %bitcast.6, s32[1,32]{1,0:T(1,128)} %bitcast.7, f32[8,2,32,512]{3,2,1,0:T(8,128)} %constant.14.clone.a_hbm, bf16[1024,512]{1,0:T(8,128)(2,1)} %constant.15.clone.bh_hbm, ...), custom_call_target="tpu_custom_call" | custom-call | tf_op jit(solution)/shard_map/pallas_call | solution.py:259
  29.4 1.7 %copy.14 = f32[4,128,128]{2,1,0:T(8,128)} copy(f32[4,128,128]{2,1,0:T(8,128)} %shard_map.118) | data formatting | bytes 524288

commit v2 on v1

--- a/solution.py
+++ b/solution.py
@@ -17,6 +17,7 @@
 CAP = 4
 TEAM = 8
 CHUNK = 16
+PARTS = 2
 
 bf16 = jnp.bfloat16
 f32 = jnp.float32
@@ -37,15 +38,16 @@
     kernel = np.fft.ifft(chirp)
     rows = (length - CROP) // 2 + np.arange(CROP)
     step = kernel[(rows[:, None] - index[None, :]) % length]
-    dealt = step.reshape(CROP // team, team, length).transpose(1, 0, 2)
-    a = np.stack([dealt.real, dealt.imag], axis=1).astype(np.float32)
+    fp = WINDOW // team // PARTS
+    dealt = step.reshape(2, PARTS, fp, team, length).transpose(3, 1, 0, 2, 4).reshape(team, PARTS, 2 * fp, length)
+    a = np.stack([dealt.real, dealt.imag], axis=2).astype(np.float32)
     st = step.T
     b = np.block([[st.real, st.imag], [-st.imag, st.real]])
     w = np.arange(WINDOW)
     ang = 2 * np.pi * ((w[:, None] * w[None, :]) % WINDOW) / WINDOW
     c, s = np.cos(ang), np.sin(ang)
     x = np.block([[c, -s], [s, c]])
-    order = w.reshape(WINDOW // team, team).T.reshape(-1)
+    order = w.reshape(PARTS, fp, team).transpose(0, 2, 1).reshape(-1)
     y = np.concatenate([c[:, order], s[:, order]], axis=0)
     return a, host_split(b), host_split(x), host_split(y)
 
@@ -76,8 +78,8 @@
            ksend, krecv, xsend, xrecv):
     length = t_ref.shape[1]
     beams, probes = phases_ref.shape
-    hold = CROP // team
-    fold = WINDOW // team
+    fold = WINDOW // team // PARTS
+    hold = 2 * fold
     m = chunk * hold
     slots = team * CAP
     sj = slots * fold
@@ -129,8 +131,37 @@
     top = rows_of(jnp.broadcast_to(place[:, 0:1], (slots, 128)))[:, 0:1]
     left = rows_of(jnp.broadcast_to(place[:, 1:2], (slots, 128)))
     j_row = lax.broadcasted_iota(jnp.int32, (sj, 1), 0) & (fold - 1)
-    first = (j_row * team + mi).astype(f32)
-    pick = j_row + jnp.where(first < top, fold, 0)
+    scale = used * (1.0 / math.sqrt(beams))
+
+    def weights(c):
+        bi = lax.broadcasted_iota(jnp.int32, (beams, m), 0)
+        bj = lax.broadcasted_iota(jnp.int32, (beams, m), 1)
+        spread = jnp.where(bi == c * chunk + bj // hold, 1.0, 0.0).astype(bf16)
+        angle = dot(level, spread) * (2.0 * math.pi / LEVELS)
+        wc = rows_of(jnp.cos(angle) * scale)
+        ws = rows_of(jnp.sin(angle) * scale)
+        for h in range(PARTS):
+            first = ((j_row + h * fold) * team + mi).astype(f32)
+            pick = j_row + jnp.where(first < top, fold, 0)
+            keep = (lax.broadcasted_iota(jnp.int32, (sj, m), 1) & (hold - 1)) == pick
+            w_hi, w_lo = split(jnp.where(keep, wc, 0.0))
+            wh[h, 0:sj] = w_hi
+            wl[h, 0:sj] = w_lo
+            w_hi, w_lo = split(jnp.where(keep, ws, 0.0))
+            wh[h, sj:] = w_hi
+            wl[h, sj:] = w_lo
+
+    def waves(c):
+        index = lax.broadcasted_iota(jnp.int32, (chunk, length), 1)
+        out = []
+        for row in (0, 4):
+            k = kbuf[pl.ds(c * chunk, chunk), row, :]
+            k = jnp.concatenate([k] * (length // 128), axis=1)
+            ang = ((k * index) & (length - 1)).astype(f32) * (2.0 * math.pi / length)
+            out += [jnp.cos(ang), jnp.sin(ang)]
+        return out
+
+    weights(0)
 
     moves[4].wait()
     t_hi, t_lo = split(t_ref[...])
@@ -141,32 +172,10 @@
     for copy in sends:
         copy.wait_recv()
 
-    def one_chunk(c, is_first):
-        bi = lax.broadcasted_iota(jnp.int32, (beams, m), 0)
-        bj = lax.broadcasted_iota(jnp.int32, (beams, m), 1)
-        spread = jnp.where(bi == c * chunk + bj // hold, 1.0, 0.0).astype(bf16)
-        angle = dot(level, spread) * (2.0 * math.pi / LEVELS)
-        scale = used * (1.0 / math.sqrt(beams))
-        keep = (lax.broadcasted_iota(jnp.int32, (sj, m), 1) & (hold - 1)) == pick
-        w_hi, w_lo = split(jnp.where(keep, rows_of(jnp.cos(angle) * scale), 0.0))
-        wh[0:sj] = w_hi
-        wl[0:sj] = w_lo
-        w_hi, w_lo = split(jnp.where(keep, rows_of(jnp.sin(angle) * scale), 0.0))
-        wh[sj:] = w_hi
-        wl[sj:] = w_lo
-
-        index = lax.broadcasted_iota(jnp.int32, (chunk, length), 1)
-
-        def wave(row):
-            k = kbuf[pl.ds(c * chunk, chunk), row, :]
-            k = jnp.concatenate([k] * (length // 128), axis=1)
-            ang = ((k * index) & (length - 1)).astype(f32) * (2.0 * math.pi / length)
-            return jnp.cos(ang)[:, None, :], jnp.sin(ang)[:, None, :]
-
-        cy, sy = wave(0)
-        cx, sx = wave(4)
-        ar = a_ref[0][None]
-        ai = a_ref[1][None]
+    def one_chunk(h, wave, is_first):
+        cy, sy, cx, sx = (v[:, None, :] for v in wave)
+        ar = a_ref[h, 0][None]
+        ai = a_ref[h, 1][None]
         lr_hi, lr_lo = split((ar * cy - ai * sy).reshape(m, length))
         li_hi, li_lo = split((ar * sy + ai * cy).reshape(m, length))
         lh[0:m, 0:length] = lr_hi
@@ -202,37 +211,42 @@
         @pl.loop(0, 2 * CROP // 256)
         def _(q):
             cols = pl.ds(pl.multiple_of(q * 256, 256), 256)
-            part = dot3(wh[...], wl[...], eh[:, cols], el[:, cols])
+            part = dot3(wh[h], wl[h], eh[:, cols], el[:, cols])
             p_buf[:, cols] = part if is_first else p_buf[:, cols] + part
 
-    one_chunk(0, True)
-    if beams > chunk:
-        @pl.loop(1, beams // chunk)
-        def _(c):
-            one_chunk(c, False)
-
-    vr = p_buf[0:sj, 0:CROP] - p_buf[sj:, CROP:]
-    vi = p_buf[0:sj, CROP:] + p_buf[sj:, 0:CROP]
-    inside = lax.broadcasted_iota(jnp.int32, (sj, WINDOW), 1).astype(f32) >= left
-    folded = jnp.concatenate(
-        [jnp.where(inside, vr[:, 0:WINDOW], vr[:, WINDOW:]),
-         jnp.where(inside, vi[:, 0:WINDOW], vi[:, WINDOW:])], axis=1)
-    f_hi, f_lo = split(folded)
-    xbuf[...] = dot3(f_hi, f_lo, xh_ref[...], xl_ref[...]).reshape(team, CAP * fold, 2 * WINDOW)
-
     copies = []
-    for e in range(1, team):
-        other = lax.rem(mi + e, team)
-        copy = pltpu.make_async_remote_copy(
-            src_ref=xbuf.at[other], dst_ref=zbuf.at[mi], send_sem=xsend.at[e - 1], recv_sem=xrecv.at[e - 1],
-            device_id={"beam": base + other}, device_id_type=MESH)
-        copy.start()
-        copies.append(copy)
-    zbuf[mi] = xbuf[mi]
+    wave = waves(0)
+    for h in range(PARTS):
+        if beams > chunk and h > 0:
+            weights(0)
+        one_chunk(h, wave, True)
+        if beams > chunk:
+            @pl.loop(1, beams // chunk)
+            def _(c):
+                weights(c)
+                one_chunk(h, waves(c), False)
+
+        vr = p_buf[0:sj, 0:CROP] - p_buf[sj:, CROP:]
+        vi = p_buf[0:sj, CROP:] + p_buf[sj:, 0:CROP]
+        inside = lax.broadcasted_iota(jnp.int32, (sj, WINDOW), 1).astype(f32) >= left
+        folded = jnp.concatenate(
+            [jnp.where(inside, vr[:, 0:WINDOW], vr[:, WINDOW:]),
+             jnp.where(inside, vi[:, 0:WINDOW], vi[:, WINDOW:])], axis=1)
+        f_hi, f_lo = split(folded)
+        xbuf[h] = dot3(f_hi, f_lo, xh_ref[...], xl_ref[...]).reshape(team, CAP * fold, 2 * WINDOW)
+        for e in range(1, team):
+            other = lax.rem(mi + e, team)
+            at = h * (team - 1) + e - 1
+            copy = pltpu.make_async_remote_copy(
+                src_ref=xbuf.at[h, other], dst_ref=zbuf.at[h, mi], send_sem=xsend.at[at], recv_sem=xrecv.at[at],
+                device_id={"beam": base + other}, device_id_type=MESH)
+            copy.start()
+            copies.append(copy)
+        zbuf[h, mi] = xbuf[h, mi]
     for copy in copies:
         copy.wait_recv()
     for k in range(CAP):
-        z = zbuf[:, k * fold:(k + 1) * fold, :].reshape(WINDOW, 2 * WINDOW)
+        z = zbuf[:, :, k * fold:(k + 1) * fold, :].reshape(WINDOW, 2 * WINDOW)
         z_hi, z_lo = split(z)
         y = dot3(yh_ref[...], yl_ref[...], z_hi, z_lo)
         yr = y[0:WINDOW, 0:WINDOW] + y[WINDOW:, WINDOW:]
@@ -251,8 +265,8 @@
         probes, beam_total = phases.shape
         chunk = math.gcd(beam_total, CHUNK)
         a, b, x, y = constants(length, team)
-        m = chunk * (CROP // team)
-        sj = CAP * WINDOW
+        m = chunk * (CROP // team // PARTS)
+        sj = CAP * WINDOW // PARTS
         t = transmission.reshape(2 * length, length)
         operands = (t, beams, phases.T, positions.T, owner.reshape(1, probes), a, *b, *x, *y)
         held = [pltpu.VMEM(v.shape[1:] if v is a else v.shape, v.dtype) for v in operands]
@@ -272,15 +286,15 @@
                 pltpu.VMEM((2 * m, length), f32),
                 pltpu.VMEM((m, 2 * CROP), bf16),
                 pltpu.VMEM((m, 2 * CROP), bf16),
-                pltpu.VMEM((2 * sj, m), bf16),
-                pltpu.VMEM((2 * sj, m), bf16),
+                pltpu.VMEM((PARTS, 2 * sj, m), bf16),
+                pltpu.VMEM((PARTS, 2 * sj, m), bf16),
                 pltpu.VMEM((2 * sj, 2 * CROP), f32),
-                pltpu.VMEM((team, CAP * WINDOW // team, 2 * WINDOW), f32),
-                pltpu.VMEM((team, CAP * WINDOW // team, 2 * WINDOW), f32),
+                pltpu.VMEM((PARTS, team, CAP * WINDOW // team // PARTS, 2 * WINDOW), f32),
+                pltpu.VMEM((PARTS, team, CAP * WINDOW // team // PARTS, 2 * WINDOW), f32),
                 pltpu.SemaphoreType.DMA((n - 1,)),
                 pltpu.SemaphoreType.DMA((n - 1,)),
-                pltpu.SemaphoreType.DMA((team - 1,)),
-                pltpu.SemaphoreType.DMA((team - 1,)),
+                pltpu.SemaphoreType.DMA((PARTS * (team - 1),)),
+                pltpu.SemaphoreType.DMA((PARTS * (team - 1),)),
             ],
             compiler_params=pltpu.CompilerParams(
                 collective_id=0, has_side_effects=True, vmem_limit_bytes=60 << 20),

time: 31.2 us -> 27.8 us (0.89); the launches traced: 31.1 us -> 27.3 us
  Pallas kernels: 29.4 us -> 25.7 us
    pallas_call x1, Pallas kernels: 29.4 us -> 25.7 us  [local(): pl.pallas_call(functools.partial(kernel, n, team, chunk), out_shape=jax.S...]
where the time goes in v2:
time: 27.8 us; the launch traced here: 27.3 us
  Pallas kernels  25.7 us (92%)
  local copies, waits for them, and re-layouts  1.67 us (6%)
    pallas_call x1, Pallas kernels, local(): pl.pallas_call(functools.partial(kernel, n, team, chunk), out_shape=jax.S...  25.7 us
    unnamed x1, local copies, waits for them, and re-layouts  1.67 us

profile of v2, /device:TPU:1, one launch (start us, length us, event | category | flops | bytes accessed | tf_op | source)
XLA Modules:
  0.0 27.3 jit_solution(12779916164376921268)
XLA Ops:
  0.0 25.7 %shard_map.118 = f32[4,128,128]{2,1,0:T(8,128)} custom-call(f32[1024,512]{1,0:T(8,128)} %bitcast.4, s32[1,2]{1,0:T(1,128)} %beams_hbm.1, s32[16,32]{1,0:T(8,128)} %bitcast.5, s32[2,32]{1,0:T(2,128)} %bitcast.6, s32[1,32]{1,0:T(1,128)} %bitcast.7, f32[8,2,2,16,512]{4,3,2,1,0:T(8,128)} %constant.14.clone.a_hbm, bf16[1024,512]{1,0:T(8,128)(2,1)} %constant.15.clone.bh_hbm, ...), custom_call_target="tpu_custom_call" | custom-call | tf_op jit(solution)/shard_map/pallas_call | solution.py:273
  25.7 1.7 %copy.14 = f32[4,128,128]{2,1,0:T(8,128)} copy(f32[4,128,128]{2,1,0:T(8,128)} %shard_map.118) | data formatting | bytes 524288

commit v3 on v2

--- a/solution.py
+++ b/solution.py
@@ -63,6 +63,20 @@
 
 def dot_t(a, b):
     return lax.dot_general(a, b, (((1,), (1,)), ((), ())), preferred_element_type=f32)
+
+
+def turn(q, n):
+    e = n // 8
+    up = q + e
+    quad = (up >> (n // 4).bit_length() - 1) & 3
+    x = ((up & (n // 4 - 1)) - e).astype(f32) * (2.0 * math.pi / n)
+    x2 = x * x
+    s = x * (1.0 + x2 * (-1 / 6 + x2 * (1 / 120 + x2 * (-1 / 5040 + x2 * (1 / 362880)))))
+    c = 1.0 + x2 * (-1 / 2 + x2 * (1 / 24 + x2 * (-1 / 720 + x2 * (1 / 40320))))
+    odd = (quad & 1) == 1
+    cos = jnp.where(odd, s, c)
+    sin = jnp.where(odd, c, s)
+    return jnp.where(((quad + 1) & 2) == 2, -cos, cos), jnp.where(quad >= 2, -sin, sin)
 
 
 def dot3(ah, al, bh, bl):
@@ -137,9 +151,9 @@
         bi = lax.broadcasted_iota(jnp.int32, (beams, m), 0)
         bj = lax.broadcasted_iota(jnp.int32, (beams, m), 1)
         spread = jnp.where(bi == c * chunk + bj // hold, 1.0, 0.0).astype(bf16)
-        angle = dot(level, spread) * (2.0 * math.pi / LEVELS)
-        wc = rows_of(jnp.cos(angle) * scale)
-        ws = rows_of(jnp.sin(angle) * scale)
+        cos, sin = turn(dot(level, spread).astype(jnp.int32), LEVELS)
+        wc = rows_of(cos * scale)
+        ws = rows_of(sin * scale)
         for h in range(PARTS):
             first = ((j_row + h * fold) * team + mi).astype(f32)
             pick = j_row + jnp.where(first < top, fold, 0)
@@ -157,8 +171,7 @@
         for row in (0, 4):
             k = kbuf[pl.ds(c * chunk, chunk), row, :]
             k = jnp.concatenate([k] * (length // 128), axis=1)
-            ang = ((k * index) & (length - 1)).astype(f32) * (2.0 * math.pi / length)
-            out += [jnp.cos(ang), jnp.sin(ang)]
+            out += turn((k * index) & (length - 1), length)
         return out
 
     weights(0)
@@ -187,9 +200,8 @@
         lh[m:, length:] = lr_hi
         ll[m:, length:] = lr_lo
 
-        @pl.loop(0, length // 256)
-        def _(q):
-            cols = pl.ds(pl.multiple_of(q * 256, 256), 256)
+        for q in range(length // 256):
+            cols = slice(q * 256, q * 256 + 256)
             s_buf[:, cols] = dot3(lh[...], ll[...], th[:, cols], tl[:, cols])
 
         sr = s_buf[0:m].reshape(chunk, hold, length)
@@ -201,16 +213,14 @@
         lh[0:m, length:] = hi
         ll[0:m, length:] = lo
 
-        @pl.loop(0, 2 * CROP // 256)
-        def _(q):
-            cols = pl.ds(pl.multiple_of(q * 256, 256), 256)
+        for q in range(2 * CROP // 256):
+            cols = slice(q * 256, q * 256 + 256)
             hi, lo = split(dot3(lh[0:m], ll[0:m], bh_ref[:, cols], bl_ref[:, cols]))
             eh[:, cols] = hi
             el[:, cols] = lo
 
-        @pl.loop(0, 2 * CROP // 256)
-        def _(q):
-            cols = pl.ds(pl.multiple_of(q * 256, 256), 256)
+        for q in range(2 * CROP // 256):
+            cols = slice(q * 256, q * 256 + 256)
             part = dot3(wh[h], wl[h], eh[:, cols], el[:, cols])
             p_buf[:, cols] = part if is_first else p_buf[:, cols] + part
 

time: 27.8 us -> 25.4 us (0.914)
  Pallas kernels: 25.7 us -> 23.3 us
    pallas_call x1, Pallas kernels: 25.7 us -> 23.3 us  [local(): pl.pallas_call(functools.partial(kernel, n, team, chunk), out_shape=jax.S...]
where the time goes in v3:
time: 25.4 us; the launch traced here: 25 us
  Pallas kernels  23.3 us (92%)
  local copies, waits for them, and re-layouts  1.67 us (7%)
    pallas_call x1, Pallas kernels, local(): pl.pallas_call(functools.partial(kernel, n, team, chunk), out_shape=jax.S...  23.3 us
    unnamed x1, local copies, waits for them, and re-layouts  1.67 us

profile of v3, /device:TPU:1, one launch (start us, length us, event | category | flops | bytes accessed | tf_op | source)
XLA Modules:
  0.0 25.0 jit_solution(3316100467121726370)
XLA Ops:
  0.0 23.3 %shard_map.118 = f32[4,128,128]{2,1,0:T(8,128)} custom-call(f32[1024,512]{1,0:T(8,128)} %bitcast.4, s32[1,2]{1,0:T(1,128)} %beams_hbm.1, s32[16,32]{1,0:T(8,128)} %bitcast.5, s32[2,32]{1,0:T(2,128)} %bitcast.6, s32[1,32]{1,0:T(1,128)} %bitcast.7, f32[8,2,2,16,512]{4,3,2,1,0:T(8,128)} %constant.14.clone.a_hbm, bf16[1024,512]{1,0:T(8,128)(2,1)} %constant.15.clone.bh_hbm, ...), custom_call_target="tpu_custom_call" | custom-call | tf_op jit(solution)/shard_map/pallas_call | solution.py:283
  23.3 1.7 %copy.14 = f32[4,128,128]{2,1,0:T(8,128)} copy(f32[4,128,128]{2,1,0:T(8,128)} %shard_map.118) | data formatting | bytes 524288
